TPU v7x, 512 devices: a whole 4x8x8 slice. The times are simulated.
512 devices in a mesh: gx: 16 (over y_lo, x), gy: 32 (over z, y_hi, core).
Axes of the slice: x: 4, y: 8 (y_hi: 2, y_lo: 4; y = y_hi * 4 + y_lo), z: 8, core: 2. Of those that a mesh axis runs over, the one named last changes fastest.
Arguments:
- right_side: float32 [2, 128, 512, 256], P(None, 'gx', 'gy'), may hold values from -6 to 6
- diagonal: float32 [128, 512, 256], P('gx', 'gy'), may hold values from 0.05 to 2
Outputs:
- solution_field: float32 [2, 128, 512, 256], P(None, 'gx', 'gy')
- residual: float32 [2, 128, 512, 256], P(None, 'gx', 'gy')
- direction: float32 [2, 128, 512, 256], P(None, 'gx', 'gy')
All inputs are finite; a program needn't handle non-finite values.
Results may differ from a plain program's by a relative error of at most 0.0003.
Values sent between devices are 32-bit elements; how exact they have to be, the bound alone decides.
No kernel may reach another device: no remote copies, remote signals or barrier semaphores. Data moves between devices by JAX's collectives and lax.ppermute only.
A program may use at most 64 MiB of HBM per device.

v0:
```python
import functools

import jax
import jax.numpy as jnp
from jax import lax
from jax.experimental import pallas as pl
from jax.experimental.pallas import tpu as pltpu
from jax.sharding import PartitionSpec as P

KX = 16
KY = 16
KZ = 8
CSWEEPS = 4
OMEGA = 0.8
HIGH = lax.Precision.HIGHEST
F32 = jnp.float32
LANES = 128
SIDE_LANE = 16
OTHER_LANE = 48
DIAG_GROUP = 12
DIAG_LANE = 96
TOTAL_LANE = 104


def dot(a, b):
    return jnp.dot(a, b, precision=HIGH, preferred_element_type=F32)


def table_dot(a, table):
    table = table.astype(jnp.bfloat16)
    out = None
    for _ in range(3):
        part = a.astype(jnp.bfloat16)
        a = a - part.astype(F32)
        product = jnp.dot(part, table, preferred_element_type=F32)
        out = product if out is None else out + product
    return out


def iota(shape, dim):
    return lax.broadcasted_iota(jnp.int32, shape, dim)


def z_sides(row):
    depth = row.shape[-1]
    lane = iota(row.shape, 1)
    before = jnp.where(lane == 0, 0.0, pltpu.roll(row, 1, 1))
    after = jnp.where(lane == depth - 1, 0.0, pltpu.roll(row, depth - 1, 1))
    return before + after


def sides(ref, r, x):
    row = ref[r, x]
    rows = row.shape[0]
    along_y = pltpu.roll(row, 1, 0) + pltpu.roll(row, rows - 1, 0)
    return ref[r, x - 1] + ref[r, x + 1] + along_y + z_sides(row)


def sweep_rows(out, field, rhs, kappa, inverse, count, shift_rhs, shift_diag):
    for r in range(2):
        for x in range(count):
            image = (6.0 + kappa(x + shift_diag)) * field[r, x + 1] - sides(field, r, x + 1)
            step = inverse(x + shift_diag) * (rhs(r, x + shift_rhs) - image)
            out[r, x] = field[r, x + 1] + step


def inverse_of(kappa):
    return jnp.where(kappa > 0.0, OMEGA / (6.0 + kappa), 0.0)


def pair_table(wide, narrow):
    return (iota((wide, narrow), 0) // 2 == iota((wide, narrow), 1)).astype(F32)


def copy_table(narrow, wide):
    return (iota((narrow, wide), 0) == iota((narrow, wide), 1) // 2).astype(F32)


def fine_pre(wide, kappa, inv, zero, guess, sums):
    for r in range(2):
        for x in range(14):
            zero[r, x] = inv(x) * wide[r, x]
    sweep_rows(guess, zero, lambda r, x: wide[r, x], kappa, inv, 12, 1, 1)
    left = []
    for r in range(2):
        rows = []
        for x in range(8):
            image = (6.0 + kappa(x + 3)) * guess[r, x + 2] - sides(guess, r, x + 2)
            rows.append(wide[r, x + 3] - image)
        left.append(rows)
    pairs = [left[r][2 * x] + left[r][2 * x + 1] for r in range(2) for x in range(4)]
    return level_rows(pairs + [kappa(2 * x + 1) + kappa(2 * x + 2) for x in range(6)], sums)


def level_rows(pairs, sums):
    table = pair_table(256, LANES)
    sums[...] = jnp.zeros(sums.shape, F32)
    for i, pair in enumerate(pairs):
        sums[pl.ds(32 * i + 4, 24), :] = table_dot(pair, table)

    def level_row(i):
        pair = sums[pl.ds(32 * i, 16, stride=2), :] + sums[pl.ds(32 * i + 1, 16, stride=2), :]
        return pair * 0.25

    return level_row


def own_rows(shape, low, high):
    row = iota(shape, 0)
    return (row >= low) & (row < high)


def own_eight(row):
    return pltpu.roll(row, 12, 0)[0:8]


def gathered_line(vectors):
    row = iota((16, LANES), 0)
    stacked = jnp.zeros((16, LANES), F32)
    for group, vector in vectors.items():
        stacked = jnp.where(row == group, vector, stacked)
    table = iota((LANES, LANES), 0) // (LANES // KZ) == iota((LANES, LANES), 1) % KZ
    spread = table_dot(stacked, table.astype(F32))
    return jnp.sum(jnp.where(iota((16, LANES), 1) // KZ == row, spread, 0.0), axis=0, keepdims=True)


def level_pre(rhs, extra, guess, zero, first, last):
    linv = [inverse_of(extra(x)) for x in range(12)]
    for r in range(2):
        for x in range(12):
            zero[r, x] = linv[x] * rhs(r, x)
    sweep_rows(guess, zero, rhs, extra, lambda x: linv[x], 10, 1, 1)
    left = []
    for r in range(2):
        rows = []
        for x in range(first, last):
            image = (6.0 + extra(x)) * guess[r, x - 1] - sides(guess, r, x - 1)
            rows.append(rhs(r, x) - image)
        left.append(rows)
    return left


def total(rows):
    out = rows[0]
    for row in rows[1:]:
        out = out + row
    return out


def fine_kernel(place, both, inv, guess, level, line, zero, sums, zero_level, guess_level):
    for x in range(14):
        inv[x] = inverse_of(both[2, x])
    level_row = fine_pre(both, lambda x: both[2, x], lambda x: inv[x], zero, guess, sums)
    own = own_rows((16, LANES), 4, 12)
    nothing = jnp.zeros((16, LANES), F32)
    rhs = [[jnp.where(own, level_row(4 * r + x), 0.0) for x in range(4)] for r in range(2)]
    extra = [level_row(8 + x) for x in range(6)]
    for r in range(2):
        for x in range(4):
            level[r, x] = own_eight(rhs[r][x])
    for x in range(4):
        level[2, x] = own_eight(extra[x + 1])
    left = level_pre(
        lambda r, x: rhs[r][x - 4] if 4 <= x < 8 else nothing,
        lambda x: extra[x - 3] if 3 <= x < 9 else nothing,
        guess_level, zero_level, 2, 10,
    )
    row = iota((16, LANES), 0)
    odd = place[1] % 2
    other = (row < 4 * (1 - odd)) | (row >= 16 - 4 * odd)
    vectors = {}
    for r in range(2):
        for side, rows in enumerate((left[r][2:6], left[r][0:2], left[r][6:8])):
            column = total(rows)
            for far in range(2):
                part = jnp.where(other, column, 0.0) if far else jnp.where(other, 0.0, column)
                vectors[(3 * far + side) * 2 + r] = jnp.sum(part, axis=0, keepdims=True)
    diag_sum = jnp.where(own, total(extra[1:5]), 0.0)
    vectors[DIAG_GROUP] = jnp.sum(diag_sum, axis=0, keepdims=True)
    line[...] = gathered_line(vectors)


def fold(field):
    folded = field[0:8] + field[8:16] + field[16:24]
    return folded[:, :LANES] + folded[:, LANES:]


def image_kernel(wide, level, first, both, inv, image, guess, narrow, line, zero, zero_level):
    for r in range(2):
        for x in range(14):
            image[r, x] = (6.0 + both[2, x]) * wide[r, x + 1] - sides(wide, r, x + 1)
            zero[r, x] = inv[x] * image[r, x]
    kappa = lambda x: both[2, x]
    sweep_rows(guess, zero, lambda r, x: image[r, x], kappa, lambda x: inv[x], 12, 1, 1)
    own = own_rows((24, 256), 4, 20)
    own_level = own_rows((16, LANES), 4, 12)
    extra = lambda x: first[2, x + 2]
    linv = [inverse_of(extra(x)) for x in range(8)]
    for r in range(2):
        for x in range(8):
            zero_level[r, x] = linv[x] * level[r, x]
    level_rhs = lambda r, x: level[r, x]
    sweep_rows(narrow, zero_level, level_rhs, extra, lambda x: linv[x], 6, 1, 1)
    vectors = {}
    totals = []
    for r in range(2):
        rz = total([both[r, x + 3] * wide[r, x + 4] for x in range(8)])
        pq = total([image[r, x + 3] * wide[r, x + 4] for x in range(8)])
        energy = None
        for x in range(8):
            back = (6.0 + both[2, x + 3]) * guess[r, x + 2] - sides(guess, r, x + 2)
            term = guess[r, x + 2] * (2.0 * image[r, x + 3] - back)
            energy = term if energy is None else energy + term
        energy = fold(jnp.where(own, energy, 0.0))
        column = None
        for x in range(4):
            back = (6.0 + extra(x + 2)) * narrow[r, x + 1] - sides(narrow, r, x + 1)
            left = level[r, x + 2] - back
            column = left if column is None else column + left
            term = narrow[r, x + 1] * (level[r, x + 2] + left)
            term = 4.0 * jnp.where(own_level, term, 0.0)
            energy = energy + term[0:8] + term[8:16]
        vectors[r] = jnp.sum(jnp.where(own_level, column, 0.0), axis=0, keepdims=True)
        totals.append((TOTAL_LANE + r, fold(jnp.where(own, rz, 0.0))))
        totals.append((TOTAL_LANE + 2 + r, fold(jnp.where(own, pq, 0.0))))
        totals.append((TOTAL_LANE + 4 + r, energy))
    out = gathered_line(vectors)
    lane = iota((1, LANES), 1)
    for place, part in totals:
        value = jnp.sum(jnp.sum(part, axis=0, keepdims=True), axis=1, keepdims=True)
        out = jnp.where(lane == place, value, out)
    line[...] = out


def coarse_rows(gathered):
    rows = [gathered[x] for x in range(KX)]
    lane = iota(rows[0].shape, 1)
    out = []
    for x in range(KX):
        row = rows[x]
        if x < KX - 1:
            row = row + pltpu.roll(rows[x + 1], LANES - SIDE_LANE, 1)
        if x > 0:
            row = row + pltpu.roll(rows[x - 1], LANES - 2 * SIDE_LANE, 1)
        out.append(jnp.where(lane < 2 * KZ, row, 0.0))
    return rows, out


def coarse_solve(rhs, diag, weights):
    weight_x, weight_y, weight_z = weights
    shape = rhs[0].shape
    row = iota(shape, 0)
    lane = iota(shape, 1) % KZ
    inverse = [OMEGA / d for d in diag]
    value = [i * b for i, b in zip(inverse, rhs)]
    nothing = jnp.zeros(shape, F32)
    for _ in range(CSWEEPS - 1):
        new = []
        for x in range(KX):
            v = value[x]
            below = value[x - 1] if x > 0 else nothing
            above = value[x + 1] if x < KX - 1 else nothing
            along_y = jnp.where(row == 0, 0.0, pltpu.roll(v, 1, 0))
            along_y = along_y + jnp.where(row == KY - 1, 0.0, pltpu.roll(v, shape[0] - 1, 0))
            along_z = jnp.where(lane == 0, 0.0, pltpu.roll(v, 1, 1))
            along_z = along_z + jnp.where(lane == KZ - 1, 0.0, pltpu.roll(v, LANES - 1, 1))
            image = diag[x] * v - (
                weight_x * (below + above) + weight_y * along_y + weight_z * along_z
            )
            new.append(v + inverse[x] * (rhs[x] - image))
        value = new
    return value


def coarse_diag_of(rows, weights):
    lane = iota(rows[0].shape, 1)
    base = 2.0 * (weights[0] + weights[1] + weights[2])
    out = []
    for row in rows:
        first = pltpu.roll(row, LANES - DIAG_LANE, 1)
        second = pltpu.roll(row, LANES - DIAG_LANE + KZ, 1)
        both = jnp.where(lane < KZ, first, jnp.where(lane < 2 * KZ, second, 0.0))
        out.append(base + both)
    return out


def up_blocks(place, value, spread, narrow, target):
    gx, gy = place[0], place[1]
    spread[...] = jnp.zeros(spread.shape, F32)
    stacked = jnp.concatenate(value, axis=0)
    lane_table = iota((LANES, LANES), 0)
    col = iota((LANES, LANES), 1) // (LANES // KZ)
    for r in range(2):
        wide = table_dot(stacked, (lane_table == r * KZ + col).astype(F32))
        for x in range(KX):
            spread[r, x + 1, pl.ds(8, KY), :] = wide[KY * x : KY * (x + 1)]
    odd = gy % 2
    low = gy // 2 + odd + 7
    row = iota((16, LANES), 0)
    limit = 4 + 8 * odd
    for r in range(2):
        for x in range(3):
            first = spread[r, gx + x, pl.ds(low, 1), :]
            second = spread[r, gx + x, pl.ds(low + 1, 1), :]
            tile = jnp.where(row < limit, first, second)
            for i in ((0, 1, 2), (3, 4, 5, 6), (7, 8, 9))[x]:
                target[r, i] = narrow[r, i] + tile


def post(place, value, spread, narrow, level_rhs, extra, guess, rhs, both, inv, s10, s8, s6, ups, f12, f10, out):
    up_blocks(place, value, spread, narrow, s10)
    linv = {x: inverse_of(extra(x)) for x in range(2, 10)}
    sweep_rows(s8, s10, level_rhs, extra, lambda x: linv[x], 8, 2, 2)
    sweep_rows(s6, s8, level_rhs, extra, lambda x: linv[x], 6, 3, 3)
    table_z = copy_table(LANES, 256)
    for r in range(2):
        for x in range(6):
            base = 32 * (6 * r + x)
            ups[pl.ds(base, 16, stride=2), :] = s6[r, x]
            ups[pl.ds(base + 1, 16, stride=2), :] = s6[r, x]
            wide = table_dot(ups[pl.ds(base + 4, 24), :], table_z)
            for i in range(2):
                f12[r, 2 * x + i] = guess[r, 2 * x + i] + wide
    kappa = lambda x: both[2, x]
    sweep_rows(f10, f12, rhs, kappa, lambda x: inv[x], 10, 2, 2)
    for r in range(2):
        for x in range(8):
            image = (6.0 + kappa(x + 3)) * f10[r, x + 1] - sides(f10, r, x + 1)
            out(r, x, f10[r, x + 1] + inv[x + 3] * (rhs(r, x + 3) - image))


def middle(row):
    return pltpu.roll(row, row.shape[0] - 4, 0)[0:16]


def share(alone, kappa, inv, image, zero, guess, sums):
    nothing = jnp.zeros((24, 256), F32)
    for r in range(2):
        for x in range(14):
            if 2 <= x < 12:
                image[r, x] = (6.0 + kappa(x)) * alone[r, x + 1] - sides(alone, r, x + 1)
                zero[r, x] = inv(x) * image[r, x]
            else:
                image[r, x] = nothing
                zero[r, x] = nothing
        for x in (0, 1, 14, 15):
            guess[r, x] = nothing
        for x in range(2, 14):
            back = (6.0 + kappa(x - 1)) * zero[r, x - 1] - sides(zero, r, x - 1)
            guess[r, x] = zero[r, x - 1] + inv(x - 1) * (image[r, x - 1] - back)
    pairs = []
    for r in range(2):
        rows = []
        for x in range(14):
            back = (6.0 + kappa(x)) * guess[r, x + 1] - sides(guess, r, x + 1)
            rows.append(image[r, x] - back)
        pairs = pairs + [rows[0]]
        pairs = pairs + [rows[2 * x + 1] + rows[2 * x + 2] for x in range(6)] + [rows[13]]
    return level_rows(pairs, sums)


def precond_kernel(weights, place, gathered, level, guess, both, inv,
                   precond, diag_out, part, low, high,
                   zero_level, narrow, alone, image, zero, guess_alone, sums,
                   spread, s10, s8, s6, ups, f12, f10):
    level_pre(lambda r, x: level[r, x], lambda x: level[2, x], narrow, zero_level, 4, 4)
    rows, rhs = coarse_rows(gathered)
    diag = coarse_diag_of(rows, weights)
    for x in range(KX):
        diag_out[x] = diag[x]
    value = coarse_solve(rhs, diag, weights)
    own = own_rows((24, 256), 4, 20)
    top = iota((8, LANES), 0) < 4
    for r in range(2):
        for x in (0, 1, 2, 3, 12, 13, 14, 15):
            alone[r, x] = jnp.zeros((24, 256), F32)

    def out(r, x, row):
        own_part = middle(row)
        precond[r, x] = own_part
        alone[r, x + 4] = jnp.where(own, row, 0.0)
        left, right = own_part[:, :LANES], own_part[:, LANES:]
        low[r, x, 0:8, :] = jnp.where(top, left[0:8], pltpu.roll(right[0:8], 4, 0))
        high[r, x, 0:8, :] = jnp.where(top, pltpu.roll(left[8:16], 4, 0), right[8:16])

    post(
        place, value, spread, narrow, lambda r, x: level[r, x], lambda x: level[2, x],
        guess, lambda r, x: both[r, x], both, inv, s10, s8, s6, ups, f12, f10, out,
    )
    level_row = share(
        alone, lambda x: both[2, x], lambda x: inv[x], image, zero, guess_alone, sums
    )
    for r in range(2):
        for x in range(8):
            row = level_row(8 * r + x)
            part[r, x] = row
            low[r, x, 8:16, :] = pltpu.roll(row, 14, 0)[0:8]
            high[r, x, 8:16, :] = row[8:16]


def final_kernel(weights, place, gathered, diag_in, narrow, level, first, guess, image, both, inv, precond, right,
                 solution_field, residual, direction, spread, s10, s8, s6, ups, f12, f10):
    rows, rhs = coarse_rows(gathered)
    diag = [diag_in[x] for x in range(KX)]
    value = coarse_solve(rhs, diag, weights)
    sums = jnp.sum(total(rows), axis=0, keepdims=True)
    product = jnp.sum(total([a * b for a, b in zip(rhs, value)]), axis=0, keepdims=True)
    line = iota(sums.shape, 1)

    def pick(row, low, high):
        return jnp.sum(jnp.where((line >= low) & (line < high), row, 0.0), axis=1, keepdims=True)

    alphas, betas = [], []
    for r in range(2):
        rz = pick(sums, TOTAL_LANE + r, TOTAL_LANE + r + 1)
        pq = pick(sums, TOTAL_LANE + 2 + r, TOTAL_LANE + 3 + r)
        energy = pick(sums, TOTAL_LANE + 4 + r, TOTAL_LANE + 5 + r)
        energy = energy + 4.0 * pick(product, r * KZ, (r + 1) * KZ)
        alpha = rz / pq
        alphas.append(alpha)
        betas.append(alpha * alpha * energy / rz - 1.0)

    def out(r, x, row):
        p = precond[r, x]
        solution_field[r, x] = alphas[r] * p
        residual[r, x] = right[r, x] - alphas[r] * middle(image[r, x + 3])
        direction[r, x] = p - alphas[r] * middle(row) + betas[r] * p

    post(
        place, value, spread, narrow, lambda r, x: level[r, x - 2], lambda x: first[2, x],
        guess, lambda r, x: image[r, x], both, inv, s10, s8, s6, ups, f12, f10, out,
    )


def call(kernel, outs, scratch, place=None):
    vmem = pl.BlockSpec(memory_space=pltpu.VMEM)

    def run(*args):
        specs = [vmem] * len(args)
        if place is not None:
            args = (place,) + args
            specs = [pl.BlockSpec(memory_space=pltpu.SMEM)] + specs
        return pl.pallas_call(
            kernel,
            out_shape=[jax.ShapeDtypeStruct(shape, F32) for shape in outs],
            in_specs=specs,
            out_specs=[vmem] * len(outs),
            scratch_shapes=[pltpu.VMEM(shape, F32) for shape in scratch],
            compiler_params=pltpu.CompilerParams(vmem_limit_bytes=16 * 1024 * 1024),
        )(*args)

    return run


def swap_y(low, high):
    count = lax.axis_size("gy")
    even = lax.axis_index("gy") % 2 == 0
    near_pairs = [(i, i + 1) for i in range(0, count, 2)]
    far_pairs = [(i, i + 1) for i in range(1, count - 1, 2)]
    near_pairs = near_pairs + [(b, a) for a, b in near_pairs]
    far_pairs = far_pairs + [(b, a) for a, b in far_pairs]
    far = lax.ppermute(jnp.where(even, low, high), "gy", far_pairs)
    near = lax.ppermute(jnp.where(even, high, low), "gy", near_pairs)
    return jnp.where(even, far, near), jnp.where(even, near, far)


def swap_x(low, high):
    count = lax.axis_size("gx")
    forward = [(i, i + 1) for i in range(count - 1)]
    backward = [(b, a) for a, b in forward]
    return lax.ppermute(high, "gx", forward), lax.ppermute(low, "gx", backward)


def extended(block, width_y, width_x, pad_y):
    low, high = swap_y(block[:, :, :width_y], block[:, :, block.shape[2] - width_y :])
    block = jnp.concatenate([low, block, high], axis=2)
    if pad_y:
        block = jnp.pad(block, ((0, 0), (0, 0), (pad_y, pad_y), (0, 0)))
    low, high = swap_x(block[:, :width_x], block[:, block.shape[1] - width_x :])
    return jnp.concatenate([low, block, high], axis=1)


def halves_to_rows(block):
    return jnp.concatenate([block[..., :LANES], block[..., LANES:]], axis=2)


def rows_to_halves(block):
    rows = block.shape[2] // 2
    return jnp.concatenate([block[:, :, :rows], block[:, :, rows:]], axis=3)


def exchange_shares(precond, part, low, high):
    low, high = swap_y(low, high)
    wide = jnp.concatenate([rows_to_halves(low[:, :, :8]), precond, rows_to_halves(high[:, :, :8])], axis=2)
    part = part + jnp.pad(low[:, :, 8:14], ((0, 0), (0, 0), (0, 10), (0, 0)))
    part = part + jnp.pad(high[:, :, 8:14], ((0, 0), (0, 0), (10, 0), (0, 0)))
    low = jnp.concatenate([halves_to_rows(wide[:, :4]), part[:, :4]], axis=2)
    high = jnp.concatenate([halves_to_rows(wide[:, 4:]), part[:, 4:]], axis=2)
    low, high = swap_x(low, high)
    wide = jnp.concatenate([rows_to_halves(low[:, :, :48]), wide, rows_to_halves(high[:, :, :48])], axis=1)
    part = jnp.concatenate([part[:, :4] + low[:, :, 48:], part[:, 4:] + high[:, :, 48:]], axis=1)
    return wide, part


def gather_all(line, beside):
    size_x = lax.axis_size("gx")
    size_y = lax.axis_size("gy")
    spread = jnp.broadcast_to(line[None], (size_y, 1, LANES))
    rows = lax.all_to_all(spread, "gy", 0, 0, tiled=True).reshape(KY, size_y // KY, LANES)
    even, odd = rows[:, 0], rows[:, 1]
    other = jnp.pad(even[1:], ((0, 1), (0, 0))) + jnp.pad(odd[:-1], ((1, 0), (0, 0)))
    other = jnp.pad(other[:, OTHER_LANE : 2 * OTHER_LANE], ((0, 0), (0, LANES - OTHER_LANE)))
    rows, beside = lax.optimization_barrier((even + odd + other, beside))
    spread = jnp.broadcast_to(rows[None], (size_x, KY, LANES))
    return lax.all_to_all(spread, "gx", 0, 0, tiled=True), beside


def local(right_side, diagonal):
    block_x = right_side.shape[1] * lax.axis_size("gx") // 2 // KX
    block_y = right_side.shape[2] * lax.axis_size("gy") // 2 // KY
    block_z = right_side.shape[3] // 2 // KZ
    weights = (float(block_y * block_z), float(block_x * block_z), float(block_x * block_y))
    place = jnp.stack([lax.axis_index("gx"), lax.axis_index("gy")]).astype(jnp.int32)

    both = extended(jnp.concatenate([right_side, diagonal[None]], axis=0), 3, 3, 1)
    inv, guess, level, line = call(
        fine_kernel,
        [(14, 24, 256), (2, 12, 24, 256), (3, 4, 8, LANES), (1, LANES)],
        [(2, 14, 24, 256), (448, LANES), (2, 12, 16, LANES), (2, 10, 16, LANES)],
        place,
    )(both)
    gathered, first = gather_all(line, extended(level, 4, 4, 0))
    post_scratch = [
        (2, KX + 2, 8 + KY + 8, LANES), (2, 10, 16, LANES), (2, 8, 16, LANES), (2, 6, 16, LANES),
        (384, LANES), (2, 12, 24, 256), (2, 10, 24, 256),
    ]
    precond, diag, part, low, high = call(
        functools.partial(precond_kernel, weights),
        [(2, 8, 16, 256), (KX, KY, LANES), (2, 8, 16, LANES), (2, 8, 16, LANES), (2, 8, 16, LANES)],
        [
            (2, 12, 16, LANES), (2, 10, 16, LANES), (2, 16, 24, 256), (2, 14, 24, 256),
            (2, 14, 24, 256), (2, 16, 24, 256), (512, LANES),
        ] + post_scratch,
        place,
    )(gathered, first, guess, both, inv)
    wide, level_q = exchange_shares(precond, part, low, high)
    image, guess_q, inner, line_q = call(
        image_kernel,
        [(2, 14, 24, 256), (2, 12, 24, 256), (2, 6, 16, LANES), (1, LANES)],
        [(2, 14, 24, 256), (2, 8, 16, LANES)],
    )(wide, level_q, first, both, inv)
    low, high = swap_x(inner[:, 2:4], inner[:, 2:4])
    gathered_q, narrow_q = gather_all(line_q, jnp.concatenate([low, inner, high], axis=1))
    return tuple(
        call(
            functools.partial(final_kernel, weights),
            [(2, 8, 16, 256)] * 3,
            post_scratch,
            place,
        )(gathered_q, diag, narrow_q, level_q, first, guess_q, image, both, inv, precond, right_side)
    )


def solution(mesh):
    placed = (P(None, "gx", "gy", None), P("gx", "gy", None))
    return jax.shard_map(
        local,
        mesh=mesh,
        in_specs=placed,
        out_specs=(P(None, "gx", "gy", None),) * 3,
        check_vma=False,
    )
```

profile of v0, /device:TPU:1, one launch (start us, length us, event | category | flops | bytes accessed | tf_op | source)
XLA Modules:
  0.0 154.0 jit_solution(5254471834084632699)
XLA Ops:
  0.6 1.1 broadcast_select_fusion.7
  1.8 8.9 %collective-permute-start.1 = (f32[3,8,3,256]{3,2,1,0:T(4,128)S(1)}, f32[3,8,3,256]{3,2,1,0:T(4,128)S(1)}, u32[]{:S(2)}, u32[]{:S(2)}) collective-permute-start(f32[3,8,3,256]{3,2,1,0:T(4,128)S(1)} %broadcast_select_fusion.6), channel_id=1, source_target_pairs={{0,1},{2,3},{4,5},{6,7},{8,9},{10,11},{12,13},{14,15},{16,17},{18,... | collective-permute-start | bytes 221192 | tf_op jit(solution)/shard_map/ppermute | solution.py:463
  10.7 2.1 %collective-permute-start = (f32[3,8,3,256]{3,2,1,0:T(4,128)S(1)}, f32[3,8,3,256]{3,2,1,0:T(4,128)S(1)}, u32[]{:S(2)}, u32[]{:S(2)}) collective-permute-start(f32[3,8,3,256]{3,2,1,0:T(4,128)S(1)} %get-tuple-element.37), channel_id=1, source_target_pairs={{1,2},{3,4},{5,6},{7,8},{9,10},{11,12},{13,14},{15,16},{17,18},{19... | collective-permute-start | bytes 221192 | tf_op jit(solution)/shard_map/ppermute | solution.py:462
  12.8 7.8 %collective-permute-done = f32[3,8,3,256]{3,2,1,0:T(4,128)S(1)} collective-permute-done((f32[3,8,3,256]{3,2,1,0:T(4,128)S(1)}, f32[3,8,3,256]{3,2,1,0:T(4,128)S(1)}, u32[]{:S(2)}, u32[]{:S(2)}) %collective-permute-start) | collective-permute-done | bytes 73760 | tf_op jit(solution)/shard_map/ppermute | solution.py:462
  21.0 1.3 collective-permute-start.2
  22.3 1.3 collective-permute-start.3
  23.7 1.5 collective-permute-done.2
  25.1 3.8 %collective-permute-done.3 = f32[3,3,24,256]{3,2,1,0:T(8,128)S(1)} collective-permute-done((f32[3,3,24,256]{3,2,1,0:T(8,128)S(1)}, f32[3,3,24,256]{3,2,1,0:T(8,128)S(1)}, u32[]{:S(2)}, u32[]{:S(2)}) %collective-permute-start.3) | collective-permute-done | bytes 221216 | tf_op jit(solution)/shard_map/ppermute | solution.py:471
  29.1 2.0 %shard_map.49 = (f32[14,24,256]{2,1,0:T(8,128)S(1)}, f32[2,12,24,256]{3,2,1,0:T(8,128)S(1)}, f32[3,4,8,128]{3,2,1,0:T(8,128)S(1)}, f32[1,128]{1,0:T(1,128)S(1)}) custom-call(s32[2]{0:T(128)S(1)} %pad_add_fusion.3.place, f32[3,14,24,256]{3,2,1,0:T(8,128)S(1)} %pad_maximum_fusion.both), custom_call_target="tpu_custom_call" | custom-call | tf_op jit(solution)/shard_map/pallas_call | solution.py:443
  31.0 6.6 %collective-permute-start.4 = (f32[3,4,4,128]{3,2,1,0:T(4,128)S(1)}, f32[3,4,4,128]{3,2,1,0:T(4,128)S(1)}, u32[]{:S(2)}, u32[]{:S(2)}) collective-permute-start(f32[3,4,4,128]{3,2,1,0:T(4,128)S(1)} %get-tuple-element.66), channel_id=1, source_target_pairs={{1,2},{3,4},{5,6},{7,8},{9,10},{11,12},{13,14},{15,16},{17,18},{19... | collective-permute-start | bytes 73736 | tf_op jit(solution)/shard_map/ppermute | solution.py:462
  37.7 1.9 %collective-permute-start.5 = (f32[3,4,4,128]{3,2,1,0:T(4,128)S(1)}, f32[3,4,4,128]{3,2,1,0:T(4,128)S(1)}, u32[]{:S(2)}, u32[]{:S(2)}) collective-permute-start(f32[3,4,4,128]{3,2,1,0:T(4,128)S(1)} %get-tuple-element.67), channel_id=1, source_target_pairs={{0,1},{2,3},{4,5},{6,7},{8,9},{10,11},{12,13},{14,15},{16,17},{18,... | collective-permute-start | bytes 73736 | tf_op jit(solution)/shard_map/ppermute | solution.py:463
  40.2 12.9 %all-to-all-start = ((f32[32,1,128]{2,1,0:T(1,128)}), f32[32,1,128]{2,1,0:T(1,128)S(1)}, u32[]{:S(2)}, u32[]{:S(2)}) async-start(f32[32,1,128]{2,1,0:T(1,128)} %broadcast_in_dim.16), calls=%async_computation | async-start | bytes 32768 | tf_op jit(solution)/shard_map/all_to_all | solution.py:509
  53.2 1.3 collective-permute-start.7
  54.5 4.0 %collective-permute-start.6 = (f32[3,4,16,128]{3,2,1,0:T(8,128)S(1)}, f32[3,4,16,128]{3,2,1,0:T(8,128)S(1)}, u32[]{:S(2)}, u32[]{:S(2)}) collective-permute-start(f32[3,4,16,128]{3,2,1,0:T(8,128)S(1)} %pad_maximum_fusion.8), channel_id=1, source_target_pairs={{0,32},{32,64},{64,96},{96,128},{128,160},{160,192},{192,224},{224... | collective-permute-start | bytes 294920 | tf_op jit(solution)/shard_map/ppermute | solution.py:471
  58.5 6.3 %all-to-all-done = f32[32,1,128]{2,1,0:T(1,128)S(1)} async-done(((f32[32,1,128]{2,1,0:T(1,128)}), f32[32,1,128]{2,1,0:T(1,128)S(1)}, u32[]{:S(2)}, u32[]{:S(2)}) %all-to-all-start) | async-done | bytes 16416 | tf_op jit(solution)/shard_map/all_to_all | solution.py:509
  64.9 16.6 %all_to_all.20.gathered = f32[16,16,128]{2,1,0:T(8,128)S(1)} all-to-all(f32[16,16,128]{2,1,0:T(8,128)S(1)} %broadcast_in_dim.34), channel_id=1, replica_groups=mesh['gx'=16,'gy'=32] {'gx'}, dimensions={0} | all-to-all | bytes 262144 | tf_op jit(solution)/shard_map/all_to_all | solution.py:515
  81.5 3.8 %shard_map.50 = (f32[2,8,16,256]{3,2,1,0:T(8,128)S(1)}, f32[16,16,128]{2,1,0:T(8,128)S(1)}, f32[2,8,16,128]{3,2,1,0:T(8,128)S(1)}, f32[2,8,16,128]{3,2,1,0:T(8,128)S(1)}, f32[2,8,16,128]{3,2,1,0:T(8,128)S(1)}) custom-call(s32[2]{0:T(128)S(1)} %pad_add_fusion.3.place, f32[16,16,128]{2,1,0:T(8,128)S(1)} %all_to_all.20.gathered, ...), custom_call_target="tpu_custom_call" | custom-call | tf_op jit(solution)/shard_map/pallas_call | solution.py:443
  85.4 9.1 %collective-permute-start.8 = (f32[2,8,16,128]{3,2,1,0:T(8,128)S(1)}, f32[2,8,16,128]{3,2,1,0:T(8,128)S(1)}, u32[]{:S(2)}, u32[]{:S(2)}) collective-permute-start(f32[2,8,16,128]{3,2,1,0:T(8,128)S(1)} %get-tuple-element.52), channel_id=1, source_target_pairs={{1,2},{3,4},{5,6},{7,8},{9,10},{11,12},{13,14},{15,16},{17,18},{19... | collective-permute-start | bytes 393224 | tf_op jit(solution)/shard_map/ppermute | solution.py:462
  94.4 1.9 %collective-permute-start.9 = (f32[2,8,16,128]{3,2,1,0:T(8,128)S(1)}, f32[2,8,16,128]{3,2,1,0:T(8,128)S(1)}, u32[]{:S(2)}, u32[]{:S(2)}) collective-permute-start(f32[2,8,16,128]{3,2,1,0:T(8,128)S(1)} %get-tuple-element.53), channel_id=1, source_target_pairs={{0,1},{2,3},{4,5},{6,7},{8,9},{10,11},{12,13},{14,15},{16,17},{18,... | collective-permute-start | bytes 393224 | tf_op jit(solution)/shard_map/ppermute | solution.py:463
  96.4 1.4 collective-permute-done.8
  98.0 1.3 collective-permute-start.11
  99.3 4.0 %collective-permute-start.10 = (f32[2,4,64,128]{3,2,1,0:T(8,128)S(1)}, f32[2,4,64,128]{3,2,1,0:T(8,128)S(1)}, u32[]{:S(2)}, u32[]{:S(2)}) collective-permute-start(f32[2,4,64,128]{3,2,1,0:T(8,128)S(1)} %pad_maximum_fusion.2), channel_id=1, source_target_pairs={{0,32},{32,64},{64,96},{96,128},{128,160},{160,192},{192,224},{224... | collective-permute-start | bytes 786440 | tf_op jit(solution)/shard_map/ppermute | solution.py:471
  103.4 4.4 %collective-permute-done.11 = f32[2,4,64,128]{3,2,1,0:T(8,128)S(1)} collective-permute-done((f32[2,4,64,128]{3,2,1,0:T(8,128)S(1)}, f32[2,4,64,128]{3,2,1,0:T(8,128)S(1)}, u32[]{:S(2)}, u32[]{:S(2)}) %collective-permute-start.11) | collective-permute-done | bytes 262176 | tf_op jit(solution)/shard_map/ppermute | solution.py:471
  107.8 0.9 collective-permute-done.10
  108.8 1.4 shard_map.51
  110.2 0.8 copy-done.1
  111.6 14.0 %all-to-all-start.2 = ((f32[32,1,128]{2,1,0:T(1,128)}), f32[32,1,128]{2,1,0:T(1,128)S(1)}, u32[]{:S(2)}, u32[]{:S(2)}) async-start(f32[32,1,128]{2,1,0:T(1,128)} %broadcast_in_dim.36), calls=%async_computation.2 | async-start | bytes 32768 | tf_op jit(solution)/shard_map/all_to_all | solution.py:509
  125.7 1.3 collective-permute-start.13
  127.0 4.7 %collective-permute-start.12 = (f32[2,2,16,128]{3,2,1,0:T(8,128)S(1)}, f32[2,2,16,128]{3,2,1,0:T(8,128)S(1)}, u32[]{:S(2)}, u32[]{:S(2)}) collective-permute-start(f32[2,2,16,128]{3,2,1,0:T(8,128)S(1)} %slice.180), channel_id=1, source_target_pairs={{0,32},{32,64},{64,96},{96,128},{128,160},{160,192},{192,224},{224... | collective-permute-start | bytes 98312 | tf_op jit(solution)/shard_map/ppermute | solution.py:471
  131.7 5.6 %all-to-all-done.2 = f32[32,1,128]{2,1,0:T(1,128)S(1)} async-done(((f32[32,1,128]{2,1,0:T(1,128)}), f32[32,1,128]{2,1,0:T(1,128)S(1)}, u32[]{:S(2)}, u32[]{:S(2)}) %all-to-all-start.2) | async-done | bytes 16416 | tf_op jit(solution)/shard_map/all_to_all | solution.py:509
  137.5 13.6 %all_to_all.21.gathered = f32[16,16,128]{2,1,0:T(8,128)S(1)} all-to-all(f32[16,16,128]{2,1,0:T(8,128)S(1)} %broadcast_in_dim.37), channel_id=1, replica_groups=mesh['gx'=16,'gy'=32] {'gx'}, dimensions={0} | all-to-all | bytes 262144 | tf_op jit(solution)/shard_map/all_to_all | solution.py:515
  151.1 2.9 %shard_map.52 = (f32[2,8,16,256]{3,2,1,0:T(8,128)}, f32[2,8,16,256]{3,2,1,0:T(8,128)}, f32[2,8,16,256]{3,2,1,0:T(8,128)}) custom-call(s32[2]{0:T(128)S(1)} %pad_add_fusion.3.place, f32[16,16,128]{2,1,0:T(8,128)S(1)} %all_to_all.21.gathered, f32[16,16,128]{2,1,0:T(8,128)S(1)} %get-tuple-element.33.diag_in, f32[2,10,16,128]{3,2,1,0:T(8,128)S(1)} %pad_maximum_fusion.4.narrow, ...), custom_call_target="tpu_custom_call" | custom-call | tf_op jit(solution)/shard_map/pallas_call | solution.py:443
  (59 shorter events, 2.4 us)
Async XLA Ops:
  1.8 19.0 %copy-start = (f32[2,8,16,256]{3,2,1,0:T(8,128)S(1)}, f32[2,8,16,256]{3,2,1,0:T(8,128)}, u32[]{:S(2)}) copy-start(f32[2,8,16,256]{3,2,1,0:T(8,128)} %right.1) | copy-start | bytes 786436
  1.8 11.1 %collective-permute-start.1 = (f32[3,8,3,256]{3,2,1,0:T(4,128)S(1)}, f32[3,8,3,256]{3,2,1,0:T(4,128)S(1)}, u32[]{:S(2)}, u32[]{:S(2)}) collective-permute-start(f32[3,8,3,256]{3,2,1,0:T(4,128)S(1)} %broadcast_select_fusion.6), channel_id=1, source_target_pairs={{0,1},{2,3},{4,5},{6,7},{8,9},{10,11},{12,13},{14,15},{16,17},{18,... | collective-permute-start | bytes 221192 | tf_op jit(solution)/shard_map/ppermute | solution.py:463
  10.7 10.0 %copy-start.3 = (f32[8,16,256]{2,1,0:T(8,128)S(1)}, f32[8,16,256]{2,1,0:T(8,128)}, u32[]{:S(2)}) copy-start(f32[8,16,256]{2,1,0:T(8,128)} %param.3) | copy-start | bytes 393220
  10.7 10.0 %collective-permute-start = (f32[3,8,3,256]{3,2,1,0:T(4,128)S(1)}, f32[3,8,3,256]{3,2,1,0:T(4,128)S(1)}, u32[]{:S(2)}, u32[]{:S(2)}) collective-permute-start(f32[3,8,3,256]{3,2,1,0:T(4,128)S(1)} %get-tuple-element.37), channel_id=1, source_target_pairs={{1,2},{3,4},{5,6},{7,8},{9,10},{11,12},{13,14},{15,16},{17,18},{19... | collective-permute-start | bytes 221192 | tf_op jit(solution)/shard_map/ppermute | solution.py:462
  21.0 4.2 %collective-permute-start.2 = (f32[3,3,24,256]{3,2,1,0:T(8,128)S(1)}, f32[3,3,24,256]{3,2,1,0:T(8,128)S(1)}, u32[]{:S(2)}, u32[]{:S(2)}) collective-permute-start(f32[3,3,24,256]{3,2,1,0:T(8,128)S(1)} %get-tuple-element.40), channel_id=1, source_target_pairs={{0,32},{32,64},{64,96},{96,128},{128,160},{160,192},{192,224},{224... | collective-permute-start | bytes 663560 | tf_op jit(solution)/shard_map/ppermute | solution.py:471
  22.3 6.7 %collective-permute-start.3 = (f32[3,3,24,256]{3,2,1,0:T(8,128)S(1)}, f32[3,3,24,256]{3,2,1,0:T(8,128)S(1)}, u32[]{:S(2)}, u32[]{:S(2)}) collective-permute-start(f32[3,3,24,256]{3,2,1,0:T(8,128)S(1)} %get-tuple-element.41), channel_id=1, source_target_pairs={{32,0},{64,32},{96,64},{128,96},{160,128},{192,160},{224,192},{256... | collective-permute-start | bytes 663560 | tf_op jit(solution)/shard_map/ppermute | solution.py:471
  31.0 22.1 %collective-permute-start.4 = (f32[3,4,4,128]{3,2,1,0:T(4,128)S(1)}, f32[3,4,4,128]{3,2,1,0:T(4,128)S(1)}, u32[]{:S(2)}, u32[]{:S(2)}) collective-permute-start(f32[3,4,4,128]{3,2,1,0:T(4,128)S(1)} %get-tuple-element.66), channel_id=1, source_target_pairs={{1,2},{3,4},{5,6},{7,8},{9,10},{11,12},{13,14},{15,16},{17,18},{19... | collective-permute-start | bytes 73736 | tf_op jit(solution)/shard_map/ppermute | solution.py:462
  37.7 15.4 %collective-permute-start.5 = (f32[3,4,4,128]{3,2,1,0:T(4,128)S(1)}, f32[3,4,4,128]{3,2,1,0:T(4,128)S(1)}, u32[]{:S(2)}, u32[]{:S(2)}) collective-permute-start(f32[3,4,4,128]{3,2,1,0:T(4,128)S(1)} %get-tuple-element.67), channel_id=1, source_target_pairs={{0,1},{2,3},{4,5},{6,7},{8,9},{10,11},{12,13},{14,15},{16,17},{18,... | collective-permute-start | bytes 73736 | tf_op jit(solution)/shard_map/ppermute | solution.py:463
  40.2 24.5 %all-to-all-start = ((f32[32,1,128]{2,1,0:T(1,128)}), f32[32,1,128]{2,1,0:T(1,128)S(1)}, u32[]{:S(2)}, u32[]{:S(2)}) async-start(f32[32,1,128]{2,1,0:T(1,128)} %broadcast_in_dim.16), calls=%async_computation | async-start | bytes 32768 | tf_op jit(solution)/shard_map/all_to_all | solution.py:509
  53.2 11.7 %collective-permute-start.7 = (f32[3,4,16,128]{3,2,1,0:T(8,128)S(1)}, f32[3,4,16,128]{3,2,1,0:T(8,128)S(1)}, u32[]{:S(2)}, u32[]{:S(2)}) collective-permute-start(f32[3,4,16,128]{3,2,1,0:T(8,128)S(1)} %pad_maximum_fusion.8), channel_id=1, source_target_pairs={{32,0},{64,32},{96,64},{128,96},{160,128},{192,160},{224,192},{256... | collective-permute-start | bytes 294920 | tf_op jit(solution)/shard_map/ppermute | solution.py:471
  54.5 10.4 %collective-permute-start.6 = (f32[3,4,16,128]{3,2,1,0:T(8,128)S(1)}, f32[3,4,16,128]{3,2,1,0:T(8,128)S(1)}, u32[]{:S(2)}, u32[]{:S(2)}) collective-permute-start(f32[3,4,16,128]{3,2,1,0:T(8,128)S(1)} %pad_maximum_fusion.8), channel_id=1, source_target_pairs={{0,32},{32,64},{64,96},{96,128},{128,160},{160,192},{192,224},{224... | collective-permute-start | bytes 294920 | tf_op jit(solution)/shard_map/ppermute | solution.py:471
  85.4 12.4 %collective-permute-start.8 = (f32[2,8,16,128]{3,2,1,0:T(8,128)S(1)}, f32[2,8,16,128]{3,2,1,0:T(8,128)S(1)}, u32[]{:S(2)}, u32[]{:S(2)}) collective-permute-start(f32[2,8,16,128]{3,2,1,0:T(8,128)S(1)} %get-tuple-element.52), channel_id=1, source_target_pairs={{1,2},{3,4},{5,6},{7,8},{9,10},{11,12},{13,14},{15,16},{17,18},{19... | collective-permute-start | bytes 393224 | tf_op jit(solution)/shard_map/ppermute | solution.py:462
  94.4 3.3 %collective-permute-start.9 = (f32[2,8,16,128]{3,2,1,0:T(8,128)S(1)}, f32[2,8,16,128]{3,2,1,0:T(8,128)S(1)}, u32[]{:S(2)}, u32[]{:S(2)}) collective-permute-start(f32[2,8,16,128]{3,2,1,0:T(8,128)S(1)} %get-tuple-element.53), channel_id=1, source_target_pairs={{0,1},{2,3},{4,5},{6,7},{8,9},{10,11},{12,13},{14,15},{16,17},{18,... | collective-permute-start | bytes 393224 | tf_op jit(solution)/shard_map/ppermute | solution.py:463
  98.0 9.8 %collective-permute-start.11 = (f32[2,4,64,128]{3,2,1,0:T(8,128)S(1)}, f32[2,4,64,128]{3,2,1,0:T(8,128)S(1)}, u32[]{:S(2)}, u32[]{:S(2)}) collective-permute-start(f32[2,4,64,128]{3,2,1,0:T(8,128)S(1)} %pad_maximum_fusion.3), channel_id=1, source_target_pairs={{32,0},{64,32},{96,64},{128,96},{160,128},{192,160},{224,192},{256... | collective-permute-start | bytes 786440 | tf_op jit(solution)/shard_map/ppermute | solution.py:471
  99.3 9.3 %collective-permute-start.10 = (f32[2,4,64,128]{3,2,1,0:T(8,128)S(1)}, f32[2,4,64,128]{3,2,1,0:T(8,128)S(1)}, u32[]{:S(2)}, u32[]{:S(2)}) collective-permute-start(f32[2,4,64,128]{3,2,1,0:T(8,128)S(1)} %pad_maximum_fusion.2), channel_id=1, source_target_pairs={{0,32},{32,64},{64,96},{96,128},{128,160},{160,192},{192,224},{224... | collective-permute-start | bytes 786440 | tf_op jit(solution)/shard_map/ppermute | solution.py:471
  110.2 0.8 copy-start.1
  111.6 25.7 %all-to-all-start.2 = ((f32[32,1,128]{2,1,0:T(1,128)}), f32[32,1,128]{2,1,0:T(1,128)S(1)}, u32[]{:S(2)}, u32[]{:S(2)}) async-start(f32[32,1,128]{2,1,0:T(1,128)} %broadcast_in_dim.36), calls=%async_computation.2 | async-start | bytes 32768 | tf_op jit(solution)/shard_map/all_to_all | solution.py:509
  125.7 11.8 %collective-permute-start.13 = (f32[2,2,16,128]{3,2,1,0:T(8,128)S(1)}, f32[2,2,16,128]{3,2,1,0:T(8,128)S(1)}, u32[]{:S(2)}, u32[]{:S(2)}) collective-permute-start(f32[2,2,16,128]{3,2,1,0:T(8,128)S(1)} %slice.180), channel_id=1, source_target_pairs={{32,0},{64,32},{96,64},{128,96},{160,128},{192,160},{224,192},{256... | collective-permute-start | bytes 98312 | tf_op jit(solution)/shard_map/ppermute | solution.py:471
  127.0 10.5 %collective-permute-start.12 = (f32[2,2,16,128]{3,2,1,0:T(8,128)S(1)}, f32[2,2,16,128]{3,2,1,0:T(8,128)S(1)}, u32[]{:S(2)}, u32[]{:S(2)}) collective-permute-start(f32[2,2,16,128]{3,2,1,0:T(8,128)S(1)} %slice.180), channel_id=1, source_target_pairs={{0,32},{32,64},{64,96},{96,128},{128,160},{160,192},{192,224},{224... | collective-permute-start | bytes 98312 | tf_op jit(solution)/shard_map/ppermute | solution.py:471
  137.3 13.8 %copy-start.2 = (f32[2,12,24,256]{3,2,1,0:T(8,128)S(1)}, f32[2,12,24,256]{3,2,1,0:T(8,128)}, u32[]{:S(2)}) copy-start(f32[2,12,24,256]{3,2,1,0:T(8,128)} %copy-done.1) | copy-start | bytes 1769476
where the time goes:
time: 155 us; the launch traced here: 154 us
  starting transfers between devices  76.7 us (49%)
  waiting for transfers between devices  31.7 us (20%)
  blocking collectives  30.1 us (19%)
  Pallas kernels  10 us (6%)
  local copies, waits for them, and re-layouts  2.29 us (1%)
  other arithmetic  2.01 us (1%)
    all_to_all x2, blocking collectives, gather_all(): return (lax.all_to_all(spread, 'gx', 0, 0, tiled=True), beside)  30.1 us
    all_to_all x2, starting transfers between devices, gather_all(): lax.all_to_all(spread, 'gy', 0, 0, tiled=True)  26.9 us
    ppermute x3, starting transfers between devices, swap_y(): far = lax.ppermute(jnp.where(even, low, high), 'gy', far_pairs)  17.8 us
    ppermute x4, starting transfers between devices, swap_x(): lax.ppermute(high, 'gx', forward)  14 us
    ppermute x3, starting transfers between devices, swap_y(): near = lax.ppermute(jnp.where(even, high, low), 'gy', near_pairs)  12.8 us
    all_to_all x2, waiting for transfers between devices, gather_all(): lax.all_to_all(spread, 'gy', 0, 0, tiled=True)  11.9 us
    pallas_call x4, Pallas kernels, run(): pl.pallas_call(kernel, out_shape=[jax.ShapeDtypeStruct(shape, F32) for sh...  10 us
    ppermute x3, waiting for transfers between devices, swap_y(): far = lax.ppermute(jnp.where(even, low, high), 'gy', far_pairs)  9.21 us
  transfers between devices with their start and end apart: 16, of which 8 were waited for; matrix products, arithmetic and copies ran while one was open for 1% of the time, Pallas kernels for 0%

commit v1 on v0

--- a/solution.py
+++ b/solution.py
@@ -56,12 +56,14 @@
     return ref[r, x - 1] + ref[r, x + 1] + along_y + z_sides(row)
 
 
-def sweep_rows(out, field, rhs, kappa, inverse, count, shift_rhs, shift_diag):
+def swept(field, rhs, inverse, r, x):
+    return (1.0 - OMEGA) * field[r, x] + inverse * (rhs + sides(field, r, x))
+
+
+def sweep_rows(out, field, rhs, inverse, count, shift):
     for r in range(2):
         for x in range(count):
-            image = (6.0 + kappa(x + shift_diag)) * field[r, x + 1] - sides(field, r, x + 1)
-            step = inverse(x + shift_diag) * (rhs(r, x + shift_rhs) - image)
-            out[r, x] = field[r, x + 1] + step
+            out[r, x] = swept(field, rhs(r, x + shift), inverse(x + shift), r, x + 1)
 
 
 def inverse_of(kappa):
@@ -80,7 +82,7 @@
     for r in range(2):
         for x in range(14):
             zero[r, x] = inv(x) * wide[r, x]
-    sweep_rows(guess, zero, lambda r, x: wide[r, x], kappa, inv, 12, 1, 1)
+    sweep_rows(guess, zero, lambda r, x: wide[r, x], inv, 12, 1)
     left = []
     for r in range(2):
         rows = []
@@ -129,7 +131,7 @@
     for r in range(2):
         for x in range(12):
             zero[r, x] = linv[x] * rhs(r, x)
-    sweep_rows(guess, zero, rhs, extra, lambda x: linv[x], 10, 1, 1)
+    sweep_rows(guess, zero, rhs, lambda x: linv[x], 10, 1)
     left = []
     for r in range(2):
         rows = []
@@ -177,7 +179,19 @@
                 vectors[(3 * far + side) * 2 + r] = jnp.sum(part, axis=0, keepdims=True)
     diag_sum = jnp.where(own, total(extra[1:5]), 0.0)
     vectors[DIAG_GROUP] = jnp.sum(diag_sum, axis=0, keepdims=True)
-    line[...] = gathered_line(vectors)
+    line[...] = jnp.broadcast_to(gathered_line(vectors)[None], line.shape)
+
+
+def pack_kernel(place, level, far, near):
+    even = place[1] % 2 == 0
+    top = iota((8, LANES), 0) < 4
+    for c in range(3):
+        for i in range(2):
+            one, two = level[c, 2 * i], level[c, 2 * i + 1]
+            low = jnp.where(top, one, pltpu.roll(two, 4, 0))
+            high = jnp.where(top, pltpu.roll(one, 4, 0), two)
+            far[c, i] = jnp.where(even, low, high)
+            near[c, i] = jnp.where(even, high, low)
 
 
 def fold(field):
@@ -185,13 +199,12 @@
     return folded[:, :LANES] + folded[:, LANES:]
 
 
-def image_kernel(wide, level, first, both, inv, image, guess, narrow, line, zero, zero_level):
+def image_kernel(wide, level, first, both, inv, image, narrow, line, zero, guess, zero_level):
     for r in range(2):
         for x in range(14):
             image[r, x] = (6.0 + both[2, x]) * wide[r, x + 1] - sides(wide, r, x + 1)
             zero[r, x] = inv[x] * image[r, x]
-    kappa = lambda x: both[2, x]
-    sweep_rows(guess, zero, lambda r, x: image[r, x], kappa, lambda x: inv[x], 12, 1, 1)
+    sweep_rows(guess, zero, lambda r, x: image[r, x], lambda x: inv[x], 12, 1)
     own = own_rows((24, 256), 4, 20)
     own_level = own_rows((16, LANES), 4, 12)
     extra = lambda x: first[2, x + 2]
@@ -200,7 +213,7 @@
         for x in range(8):
             zero_level[r, x] = linv[x] * level[r, x]
     level_rhs = lambda r, x: level[r, x]
-    sweep_rows(narrow, zero_level, level_rhs, extra, lambda x: linv[x], 6, 1, 1)
+    sweep_rows(narrow, zero_level, level_rhs, lambda x: linv[x], 6, 1)
     vectors = {}
     totals = []
     for r in range(2):
@@ -229,7 +242,7 @@
     for place, part in totals:
         value = jnp.sum(jnp.sum(part, axis=0, keepdims=True), axis=1, keepdims=True)
         out = jnp.where(lane == place, value, out)
-    line[...] = out
+    line[...] = jnp.broadcast_to(out[None], line.shape)
 
 
 def coarse_rows(gathered):
@@ -307,11 +320,11 @@
                 target[r, i] = narrow[r, i] + tile
 
 
-def post(place, value, spread, narrow, level_rhs, extra, guess, rhs, both, inv, s10, s8, s6, ups, f12, f10, out):
+def post(place, value, spread, narrow, level_rhs, extra, guess, rhs, inv, s10, s8, s6, ups, f12, f10, out):
     up_blocks(place, value, spread, narrow, s10)
     linv = {x: inverse_of(extra(x)) for x in range(2, 10)}
-    sweep_rows(s8, s10, level_rhs, extra, lambda x: linv[x], 8, 2, 2)
-    sweep_rows(s6, s8, level_rhs, extra, lambda x: linv[x], 6, 3, 3)
+    sweep_rows(s8, s10, level_rhs, lambda x: linv[x], 8, 2)
+    sweep_rows(s6, s8, level_rhs, lambda x: linv[x], 6, 3)
     table_z = copy_table(LANES, 256)
     for r in range(2):
         for x in range(6):
@@ -321,12 +334,10 @@
             wide = table_dot(ups[pl.ds(base + 4, 24), :], table_z)
             for i in range(2):
                 f12[r, 2 * x + i] = guess[r, 2 * x + i] + wide
-    kappa = lambda x: both[2, x]
-    sweep_rows(f10, f12, rhs, kappa, lambda x: inv[x], 10, 2, 2)
+    sweep_rows(f10, f12, rhs, lambda x: inv[x], 10, 2)
     for r in range(2):
         for x in range(8):
-            image = (6.0 + kappa(x + 3)) * f10[r, x + 1] - sides(f10, r, x + 1)
-            out(r, x, f10[r, x + 1] + inv[x + 3] * (rhs(r, x + 3) - image))
+            out(r, x, swept(f10, rhs(r, x + 3), inv[x + 3], r, x + 1))
 
 
 def middle(row):
@@ -346,8 +357,7 @@
         for x in (0, 1, 14, 15):
             guess[r, x] = nothing
         for x in range(2, 14):
-            back = (6.0 + kappa(x - 1)) * zero[r, x - 1] - sides(zero, r, x - 1)
-            guess[r, x] = zero[r, x - 1] + inv(x - 1) * (image[r, x - 1] - back)
+            guess[r, x] = swept(zero, image[r, x - 1], inv(x - 1), r, x - 1)
     pairs = []
     for r in range(2):
         rows = []
@@ -385,7 +395,7 @@
 
     post(
         place, value, spread, narrow, lambda r, x: level[r, x], lambda x: level[2, x],
-        guess, lambda r, x: both[r, x], both, inv, s10, s8, s6, ups, f12, f10, out,
+        guess, lambda r, x: both[r, x], inv, s10, s8, s6, ups, f12, f10, out,
     )
     level_row = share(
         alone, lambda x: both[2, x], lambda x: inv[x], image, zero, guess_alone, sums
@@ -398,8 +408,12 @@
             high[r, x, 8:16, :] = row[8:16]
 
 
-def final_kernel(weights, place, gathered, diag_in, narrow, level, first, guess, image, both, inv, precond, right,
-                 solution_field, residual, direction, spread, s10, s8, s6, ups, f12, f10):
+def final_kernel(weights, place, gathered, diag_in, narrow, level, first, image, inv, precond, right,
+                 solution_field, residual, direction, zero, guess, spread, s10, s8, s6, ups, f12, f10):
+    for r in range(2):
+        for x in range(14):
+            zero[r, x] = inv[x] * image[r, x]
+    sweep_rows(guess, zero, lambda r, x: image[r, x], lambda x: inv[x], 12, 1)
     rows, rhs = coarse_rows(gathered)
     diag = [diag_in[x] for x in range(KX)]
     value = coarse_solve(rhs, diag, weights)
@@ -428,11 +442,11 @@
 
     post(
         place, value, spread, narrow, lambda r, x: level[r, x - 2], lambda x: first[2, x],
-        guess, lambda r, x: image[r, x], both, inv, s10, s8, s6, ups, f12, f10, out,
+        guess, lambda r, x: image[r, x], inv, s10, s8, s6, ups, f12, f10, out,
     )
 
 
-def call(kernel, outs, scratch, place=None):
+def call(kernel, outs, scratch, place=None, cost=None):
     vmem = pl.BlockSpec(memory_space=pltpu.VMEM)
 
     def run(*args):
@@ -446,21 +460,23 @@
             in_specs=specs,
             out_specs=[vmem] * len(outs),
             scratch_shapes=[pltpu.VMEM(shape, F32) for shape in scratch],
+            cost_estimate=cost,
             compiler_params=pltpu.CompilerParams(vmem_limit_bytes=16 * 1024 * 1024),
         )(*args)
 
     return run
 
 
-def swap_y(low, high):
+def swap_y(low, high, packed=False):
     count = lax.axis_size("gy")
     even = lax.axis_index("gy") % 2 == 0
     near_pairs = [(i, i + 1) for i in range(0, count, 2)]
     far_pairs = [(i, i + 1) for i in range(1, count - 1, 2)]
     near_pairs = near_pairs + [(b, a) for a, b in near_pairs]
     far_pairs = far_pairs + [(b, a) for a, b in far_pairs]
-    far = lax.ppermute(jnp.where(even, low, high), "gy", far_pairs)
-    near = lax.ppermute(jnp.where(even, high, low), "gy", near_pairs)
+    far, near = (low, high) if packed else (jnp.where(even, low, high), jnp.where(even, high, low))
+    far = lax.ppermute(far, "gy", far_pairs)
+    near = lax.ppermute(near, "gy", near_pairs)
     return jnp.where(even, far, near), jnp.where(even, near, far)
 
 
@@ -471,13 +487,23 @@
     return lax.ppermute(high, "gx", forward), lax.ppermute(low, "gx", backward)
 
 
-def extended(block, width_y, width_x, pad_y):
-    low, high = swap_y(block[:, :, :width_y], block[:, :, block.shape[2] - width_y :])
+def extended_x(block, width):
+    low, high = swap_x(block[:, :width], block[:, block.shape[1] - width :])
+    return jnp.concatenate([low, block, high], axis=1)
+
+
+def extended(block):
+    low, high = swap_y(block[:, :, :3], block[:, :, block.shape[2] - 3 :])
     block = jnp.concatenate([low, block, high], axis=2)
-    if pad_y:
-        block = jnp.pad(block, ((0, 0), (0, 0), (pad_y, pad_y), (0, 0)))
-    low, high = swap_x(block[:, :width_x], block[:, block.shape[1] - width_x :])
-    return jnp.concatenate([low, block, high], axis=1)
+    return extended_x(jnp.pad(block, ((0, 0), (0, 0), (1, 1), (0, 0))), 3)
+
+
+def extended_level(level, place):
+    cost = pl.CostEstimate(flops=0, bytes_accessed=16 * 1024 * 1024, transcendentals=0)
+    far, near = call(pack_kernel, [(3, 2, 8, LANES)] * 2, [], place, cost)(level)
+    low, high = swap_y(far, near, True)
+    shape = (3, 4, 4, LANES)
+    return extended_x(jnp.concatenate([low.reshape(shape), level, high.reshape(shape)], axis=2), 4)
 
 
 def halves_to_rows(block):
@@ -502,15 +528,16 @@
     return wide, part
 
 
-def gather_all(line, beside):
+def gather_all(line, beside=None):
     size_x = lax.axis_size("gx")
     size_y = lax.axis_size("gy")
-    spread = jnp.broadcast_to(line[None], (size_y, 1, LANES))
-    rows = lax.all_to_all(spread, "gy", 0, 0, tiled=True).reshape(KY, size_y // KY, LANES)
+    rows = lax.all_to_all(line, "gy", 0, 0, tiled=True).reshape(KY, size_y // KY, LANES)
     even, odd = rows[:, 0], rows[:, 1]
     other = jnp.pad(even[1:], ((0, 1), (0, 0))) + jnp.pad(odd[:-1], ((1, 0), (0, 0)))
     other = jnp.pad(other[:, OTHER_LANE : 2 * OTHER_LANE], ((0, 0), (0, LANES - OTHER_LANE)))
-    rows, beside = lax.optimization_barrier((even + odd + other, beside))
+    rows = even + odd + other
+    if beside is not None:
+        rows, beside = lax.optimization_barrier((rows, beside))
     spread = jnp.broadcast_to(rows[None], (size_x, KY, LANES))
     return lax.all_to_all(spread, "gx", 0, 0, tiled=True), beside
 
@@ -519,17 +546,19 @@
     block_x = right_side.shape[1] * lax.axis_size("gx") // 2 // KX
     block_y = right_side.shape[2] * lax.axis_size("gy") // 2 // KY
     block_z = right_side.shape[3] // 2 // KZ
+    size_y = lax.axis_size("gy")
     weights = (float(block_y * block_z), float(block_x * block_z), float(block_x * block_y))
     place = jnp.stack([lax.axis_index("gx"), lax.axis_index("gy")]).astype(jnp.int32)
 
-    both = extended(jnp.concatenate([right_side, diagonal[None]], axis=0), 3, 3, 1)
+    both = extended(jnp.concatenate([right_side, diagonal[None]], axis=0))
     inv, guess, level, line = call(
         fine_kernel,
-        [(14, 24, 256), (2, 12, 24, 256), (3, 4, 8, LANES), (1, LANES)],
+        [(14, 24, 256), (2, 12, 24, 256), (3, 4, 8, LANES), (size_y, 1, LANES)],
         [(2, 14, 24, 256), (448, LANES), (2, 12, 16, LANES), (2, 10, 16, LANES)],
         place,
     )(both)
-    gathered, first = gather_all(line, extended(level, 4, 4, 0))
+    gathered, _ = gather_all(line)
+    first = extended_level(level, place)
     post_scratch = [
         (2, KX + 2, 8 + KY + 8, LANES), (2, 10, 16, LANES), (2, 8, 16, LANES), (2, 6, 16, LANES),
         (384, LANES), (2, 12, 24, 256), (2, 10, 24, 256),
@@ -544,10 +573,10 @@
         place,
     )(gathered, first, guess, both, inv)
     wide, level_q = exchange_shares(precond, part, low, high)
-    image, guess_q, inner, line_q = call(
+    image, inner, line_q = call(
         image_kernel,
-        [(2, 14, 24, 256), (2, 12, 24, 256), (2, 6, 16, LANES), (1, LANES)],
-        [(2, 14, 24, 256), (2, 8, 16, LANES)],
+        [(2, 14, 24, 256), (2, 6, 16, LANES), (size_y, 1, LANES)],
+        [(2, 14, 24, 256), (2, 12, 24, 256), (2, 8, 16, LANES)],
     )(wide, level_q, first, both, inv)
     low, high = swap_x(inner[:, 2:4], inner[:, 2:4])
     gathered_q, narrow_q = gather_all(line_q, jnp.concatenate([low, inner, high], axis=1))
@@ -555,9 +584,9 @@
         call(
             functools.partial(final_kernel, weights),
             [(2, 8, 16, 256)] * 3,
-            post_scratch,
+            [(2, 14, 24, 256), (2, 12, 24, 256)] + post_scratch,
             place,
-        )(gathered_q, diag, narrow_q, level_q, first, guess_q, image, both, inv, precond, right_side)
+        )(gathered_q, diag, narrow_q, level_q, first, image, inv, precond, right_side)
     )
 
 

time: 155 us -> 155 us (level)
  waiting for transfers between devices: 31.7 us -> 41.1 us
  blocking collectives: 30.1 us -> 22.4 us
  starting transfers between devices: 76.7 us -> 74.7 us
  Pallas kernels: 10 us -> 11.8 us
    all_to_all x2 -> x1, blocking collectives: 30.1 us -> 22.4 us  [gather_all(): return (lax.all_to_all(spread, 'gx', 0, 0, tiled=True), beside)]
    all_to_all x2 -> x3, waiting for transfers between devices: 11.9 us -> 18.1 us  [the longest x2 17.2 us: gather_all(): lax.all_to_all(line, 'gy', 0, 0, tiled=True)]
    ppermute x6, starting transfers between devices: 30.6 us -> 25.9 us  [the longest x3 13.1 us: swap_y(): far = lax.ppermute(far, 'gy', far_pairs)]
    all_to_all x2 -> x3, starting transfers between devices: 26.9 us -> 29.6 us  [the longest x2 20.7 us: gather_all(): lax.all_to_all(line, 'gy', 0, 0, tiled=True)]
    ppermute x6, waiting for transfers between devices: 9.22 us -> 11.8 us  [the longest x3 11.7 us: swap_y(): far = lax.ppermute(far, 'gy', far_pairs)]
    pallas_call x4 -> x5, Pallas kernels: 10 us -> 11.8 us  [run(): pl.pallas_call(kernel, out_shape=[jax.ShapeDtypeStruct(shape, F32) for sh...]
    ppermute x4, waiting for transfers between devices: 2.36 us -> 3.92 us  [swap_x(): lax.ppermute(high, 'gx', forward)]
  transfers between devices with their start and end apart: 16 -> 17, of which waited for: 8 -> 11; matrix products, arithmetic and copies ran while one was open for 1% -> 0% of each run, Pallas kernels for 0% -> 0%
where the time goes in v1:
time: 155 us; the launch traced here: 154 us
  starting transfers between devices  74.7 us (48%)
  waiting for transfers between devices  41.1 us (27%)
  blocking collectives  22.4 us (14%)
  Pallas kernels  11.8 us (8%)
  other arithmetic  2 us (1%)
    all_to_all x1, blocking collectives, gather_all(): return (lax.all_to_all(spread, 'gx', 0, 0, tiled=True), beside)  22.4 us
    all_to_all x2, starting transfers between devices, gather_all(): lax.all_to_all(line, 'gy', 0, 0, tiled=True)  20.7 us
    all_to_all x2, waiting for transfers between devices, gather_all(): lax.all_to_all(line, 'gy', 0, 0, tiled=True)  17.2 us
    ppermute x4, starting transfers between devices, swap_x(): lax.ppermute(high, 'gx', forward)  14 us
    ppermute x3, starting transfers between devices, swap_y(): far = lax.ppermute(far, 'gy', far_pairs)  13.1 us
    ppermute x3, starting transfers between devices, swap_y(): near = lax.ppermute(near, 'gy', near_pairs)  12.8 us
    pallas_call x5, Pallas kernels, run(): pl.pallas_call(kernel, out_shape=[jax.ShapeDtypeStruct(shape, F32) for sh...  11.8 us
    ppermute x3, waiting for transfers between devices, swap_y(): far = lax.ppermute(far, 'gy', far_pairs)  11.7 us
  transfers between devices with their start and end apart: 17, of which 11 were waited for; matrix products, arithmetic and copies ran while one was open for 0% of the time, Pallas kernels for 0%

profile of v1, /device:TPU:1, one launch (start us, length us, event | category | flops | bytes accessed | tf_op | source)
XLA Modules:
  0.0 154.1 jit_solution(9075993308295277942)
XLA Ops:
  0.6 1.1 broadcast_select_fusion.7
  1.8 8.9 %collective-permute-start.1 = (f32[3,8,3,256]{3,2,1,0:T(4,128)S(1)}, f32[3,8,3,256]{3,2,1,0:T(4,128)S(1)}, u32[]{:S(2)}, u32[]{:S(2)}) collective-permute-start(f32[3,8,3,256]{3,2,1,0:T(4,128)S(1)} %broadcast_select_fusion.6), channel_id=1, source_target_pairs={{0,1},{2,3},{4,5},{6,7},{8,9},{10,11},{12,13},{14,15},{16,17},{18,... | collective-permute-start | bytes 221192 | tf_op jit(solution)/shard_map/ppermute | solution.py:479
  10.7 2.1 %collective-permute-start = (f32[3,8,3,256]{3,2,1,0:T(4,128)S(1)}, f32[3,8,3,256]{3,2,1,0:T(4,128)S(1)}, u32[]{:S(2)}, u32[]{:S(2)}) collective-permute-start(f32[3,8,3,256]{3,2,1,0:T(4,128)S(1)} %get-tuple-element.35), channel_id=1, source_target_pairs={{1,2},{3,4},{5,6},{7,8},{9,10},{11,12},{13,14},{15,16},{17,18},{19... | collective-permute-start | bytes 221192 | tf_op jit(solution)/shard_map/ppermute | solution.py:478
  12.8 7.8 %collective-permute-done = f32[3,8,3,256]{3,2,1,0:T(4,128)S(1)} collective-permute-done((f32[3,8,3,256]{3,2,1,0:T(4,128)S(1)}, f32[3,8,3,256]{3,2,1,0:T(4,128)S(1)}, u32[]{:S(2)}, u32[]{:S(2)}) %collective-permute-start) | collective-permute-done | bytes 73760 | tf_op jit(solution)/shard_map/ppermute | solution.py:478
  21.0 1.3 collective-permute-start.2
  22.3 1.3 collective-permute-start.3
  23.7 1.5 collective-permute-done.2
  25.1 3.8 %collective-permute-done.3 = f32[3,3,24,256]{3,2,1,0:T(8,128)S(1)} collective-permute-done((f32[3,3,24,256]{3,2,1,0:T(8,128)S(1)}, f32[3,3,24,256]{3,2,1,0:T(8,128)S(1)}, u32[]{:S(2)}, u32[]{:S(2)}) %collective-permute-start.3) | collective-permute-done | bytes 221216 | tf_op jit(solution)/shard_map/ppermute | solution.py:487
  29.1 2.6 %shard_map.49 = (f32[14,24,256]{2,1,0:T(8,128)S(1)}, f32[2,12,24,256]{3,2,1,0:T(8,128)S(1)}, f32[3,4,8,128]{3,2,1,0:T(8,128)S(1)}, f32[32,1,128]{2,1,0:T(1,128)}) custom-call(s32[2]{0:T(128)S(1)} %pad_add_fusion.3.place, f32[3,14,24,256]{3,2,1,0:T(8,128)S(1)} %pad_maximum_fusion.both), custom_call_target="tpu_custom_call" | custom-call | tf_op jit(solution)/shard_map/pallas_call | solution.py:457
  32.2 6.6 %collective-permute-start.4 = (f32[3,2,8,128]{3,2,1,0:T(8,128)S(1)}, f32[3,2,8,128]{3,2,1,0:T(8,128)S(1)}, u32[]{:S(2)}, u32[]{:S(2)}) collective-permute-start(f32[3,2,8,128]{3,2,1,0:T(8,128)S(1)} %get-tuple-element.21), channel_id=1, source_target_pairs={{1,2},{3,4},{5,6},{7,8},{9,10},{11,12},{13,14},{15,16},{17,18},{19... | collective-permute-start | bytes 73736 | tf_op jit(solution)/shard_map/ppermute | solution.py:478
  38.8 1.9 %collective-permute-start.5 = (f32[3,2,8,128]{3,2,1,0:T(8,128)S(1)}, f32[3,2,8,128]{3,2,1,0:T(8,128)S(1)}, u32[]{:S(2)}, u32[]{:S(2)}) collective-permute-start(f32[3,2,8,128]{3,2,1,0:T(8,128)S(1)} %get-tuple-element.22), channel_id=1, source_target_pairs={{0,1},{2,3},{4,5},{6,7},{8,9},{10,11},{12,13},{14,15},{16,17},{18,... | collective-permute-start | bytes 73736 | tf_op jit(solution)/shard_map/ppermute | solution.py:479
  40.8 12.9 %all-to-all-start = ((f32[32,1,128]{2,1,0:T(1,128)}), f32[32,1,128]{2,1,0:T(1,128)S(1)}, u32[]{:S(2)}, u32[]{:S(2)}) async-start(f32[32,1,128]{2,1,0:T(1,128)} %get-tuple-element.19), calls=%async_computation | async-start | bytes 32768 | tf_op jit(solution)/shard_map/all_to_all | solution.py:534
  53.7 11.6 %all-to-all-done = f32[32,1,128]{2,1,0:T(1,128)S(1)} async-done(((f32[32,1,128]{2,1,0:T(1,128)}), f32[32,1,128]{2,1,0:T(1,128)S(1)}, u32[]{:S(2)}, u32[]{:S(2)}) %all-to-all-start) | async-done | bytes 16416 | tf_op jit(solution)/shard_map/all_to_all | solution.py:534
  66.1 8.9 %all-to-all-start.1 = ((f32[16,16,128]{2,1,0:T(8,128)}), f32[16,16,128]{2,1,0:T(8,128)S(1)}, u32[]{:S(2)}, u32[]{:S(2)}) async-start(f32[16,16,128]{2,1,0:T(8,128)} %broadcast_in_dim.7), calls=%async_computation.1 | async-start | bytes 262144 | tf_op jit(solution)/shard_map/all_to_all | solution.py:542
  75.1 1.3 collective-permute-start.7
  76.4 4.0 %collective-permute-start.6 = (f32[3,4,16,128]{3,2,1,0:T(8,128)S(1)}, f32[3,4,16,128]{3,2,1,0:T(8,128)S(1)}, u32[]{:S(2)}, u32[]{:S(2)}) collective-permute-start(f32[3,4,16,128]{3,2,1,0:T(8,128)S(1)} %pad_maximum_fusion.8), channel_id=1, source_target_pairs={{0,32},{32,64},{64,96},{96,128},{128,160},{160,192},{192,224},{224... | collective-permute-start | bytes 294920 | tf_op jit(solution)/shard_map/ppermute | solution.py:487
  80.4 1.0 collective-permute-done.7
  82.9 3.7 %shard_map.51 = (f32[2,8,16,256]{3,2,1,0:T(8,128)S(1)}, f32[16,16,128]{2,1,0:T(8,128)S(1)}, f32[2,8,16,128]{3,2,1,0:T(8,128)S(1)}, f32[2,8,16,128]{3,2,1,0:T(8,128)S(1)}, f32[2,8,16,128]{3,2,1,0:T(8,128)S(1)}) custom-call(s32[2]{0:T(128)S(1)} %pad_add_fusion.3.place, f32[16,16,128]{2,1,0:T(8,128)S(1)} %all-to-all-done.1.gathered, ...), custom_call_target="tpu_custom_call" | custom-call | tf_op jit(solution)/shard_map/pallas_call | solution.py:457
  86.6 4.4 %collective-permute-start.8 = (f32[2,8,16,128]{3,2,1,0:T(8,128)S(1)}, f32[2,8,16,128]{3,2,1,0:T(8,128)S(1)}, u32[]{:S(2)}, u32[]{:S(2)}) collective-permute-start(f32[2,8,16,128]{3,2,1,0:T(8,128)S(1)} %get-tuple-element.50), channel_id=1, source_target_pairs={{1,2},{3,4},{5,6},{7,8},{9,10},{11,12},{13,14},{15,16},{17,18},{19... | collective-permute-start | bytes 393224 | tf_op jit(solution)/shard_map/ppermute | solution.py:478
  90.9 1.9 %collective-permute-start.9 = (f32[2,8,16,128]{3,2,1,0:T(8,128)S(1)}, f32[2,8,16,128]{3,2,1,0:T(8,128)S(1)}, u32[]{:S(2)}, u32[]{:S(2)}) collective-permute-start(f32[2,8,16,128]{3,2,1,0:T(8,128)S(1)} %get-tuple-element.51), channel_id=1, source_target_pairs={{0,1},{2,3},{4,5},{6,7},{8,9},{10,11},{12,13},{14,15},{16,17},{18,... | collective-permute-start | bytes 393224 | tf_op jit(solution)/shard_map/ppermute | solution.py:479
  92.9 3.9 %collective-permute-done.8 = f32[2,8,16,128]{3,2,1,0:T(8,128)S(1)} collective-permute-done((f32[2,8,16,128]{3,2,1,0:T(8,128)S(1)}, f32[2,8,16,128]{3,2,1,0:T(8,128)S(1)}, u32[]{:S(2)}, u32[]{:S(2)}) %collective-permute-start.8) | collective-permute-done | bytes 131104 | tf_op jit(solution)/shard_map/ppermute | solution.py:478
  97.0 1.3 collective-permute-start.11
  98.4 4.0 %collective-permute-start.10 = (f32[2,4,64,128]{3,2,1,0:T(8,128)S(1)}, f32[2,4,64,128]{3,2,1,0:T(8,128)S(1)}, u32[]{:S(2)}, u32[]{:S(2)}) collective-permute-start(f32[2,4,64,128]{3,2,1,0:T(8,128)S(1)} %pad_maximum_fusion.2), channel_id=1, source_target_pairs={{0,32},{32,64},{64,96},{96,128},{128,160},{160,192},{192,224},{224... | collective-permute-start | bytes 786440 | tf_op jit(solution)/shard_map/ppermute | solution.py:487
  102.4 2.6 %collective-permute-done.11 = f32[2,4,64,128]{3,2,1,0:T(8,128)S(1)} collective-permute-done((f32[2,4,64,128]{3,2,1,0:T(8,128)S(1)}, f32[2,4,64,128]{3,2,1,0:T(8,128)S(1)}, u32[]{:S(2)}, u32[]{:S(2)}) %collective-permute-start.11) | collective-permute-done | bytes 262176 | tf_op jit(solution)/shard_map/ppermute | solution.py:487
  105.0 1.8 %collective-permute-done.10 = f32[2,4,64,128]{3,2,1,0:T(8,128)S(1)} collective-permute-done((f32[2,4,64,128]{3,2,1,0:T(8,128)S(1)}, f32[2,4,64,128]{3,2,1,0:T(8,128)S(1)}, u32[]{:S(2)}, u32[]{:S(2)}) %collective-permute-start.10) | collective-permute-done | bytes 262176 | tf_op jit(solution)/shard_map/ppermute | solution.py:487
  106.9 1.9 %shard_map.52 = (f32[2,14,24,256]{3,2,1,0:T(8,128)S(1)}, f32[2,6,16,128]{3,2,1,0:T(8,128)S(1)}, f32[32,1,128]{2,1,0:T(1,128)}) custom-call(f32[2,16,24,256]{3,2,1,0:T(8,128)S(1)} %maximum_maximum_fusion.wide, f32[2,8,16,128]{3,2,1,0:T(8,128)S(1)} %pad_maximum_fusion.5.level, f32[3,12,16,128]{3,2,1,0:T(8,128)S(1)} %pad_maximum_fusion.1.level.first, ...), custom_call_target="tpu_custom_call" | custom-call | tf_op jit(solution)/shard_map/pallas_call | solution.py:457
  108.8 7.8 %all-to-all-start.2 = ((f32[32,1,128]{2,1,0:T(1,128)}), f32[32,1,128]{2,1,0:T(1,128)S(1)}, u32[]{:S(2)}, u32[]{:S(2)}) async-start(f32[32,1,128]{2,1,0:T(1,128)} %get-tuple-element.29), calls=%async_computation.2 | async-start | bytes 32768 | tf_op jit(solution)/shard_map/all_to_all | solution.py:534
  116.7 1.3 collective-permute-start.13
  118.0 4.7 %collective-permute-start.12 = (f32[2,2,16,128]{3,2,1,0:T(8,128)S(1)}, f32[2,2,16,128]{3,2,1,0:T(8,128)S(1)}, u32[]{:S(2)}, u32[]{:S(2)}) collective-permute-start(f32[2,2,16,128]{3,2,1,0:T(8,128)S(1)} %slice.172), channel_id=1, source_target_pairs={{0,32},{32,64},{64,96},{96,128},{128,160},{160,192},{192,224},{224... | collective-permute-start | bytes 98312 | tf_op jit(solution)/shard_map/ppermute | solution.py:487
  122.7 5.6 %all-to-all-done.2 = f32[32,1,128]{2,1,0:T(1,128)S(1)} async-done(((f32[32,1,128]{2,1,0:T(1,128)}), f32[32,1,128]{2,1,0:T(1,128)S(1)}, u32[]{:S(2)}, u32[]{:S(2)}) %all-to-all-start.2) | async-done | bytes 16416 | tf_op jit(solution)/shard_map/all_to_all | solution.py:534
  128.5 22.4 %all_to_all.20.gathered = f32[16,16,128]{2,1,0:T(8,128)S(1)} all-to-all(f32[16,16,128]{2,1,0:T(8,128)S(1)} %broadcast_in_dim.8), channel_id=1, replica_groups=mesh['gx'=16,'gy'=32] {'gx'}, dimensions={0} | all-to-all | bytes 262144 | tf_op jit(solution)/shard_map/all_to_all | solution.py:542
  150.9 3.2 %shard_map.53 = (f32[2,8,16,256]{3,2,1,0:T(8,128)}, f32[2,8,16,256]{3,2,1,0:T(8,128)}, f32[2,8,16,256]{3,2,1,0:T(8,128)}) custom-call(s32[2]{0:T(128)S(1)} %pad_add_fusion.3.place, f32[16,16,128]{2,1,0:T(8,128)S(1)} %all_to_all.20.gathered, f32[16,16,128]{2,1,0:T(8,128)S(1)} %get-tuple-element.32.diag_in, f32[2,10,16,128]{3,2,1,0:T(8,128)S(1)} %pad_maximum_fusion.4.narrow, ...), custom_call_target="tpu_custom_call" | custom-call | tf_op jit(solution)/shard_map/pallas_call | solution.py:457
  (54 shorter events, 3.9 us)
Async XLA Ops:
  1.8 19.0 %copy-start = (f32[2,8,16,256]{3,2,1,0:T(8,128)S(1)}, f32[2,8,16,256]{3,2,1,0:T(8,128)}, u32[]{:S(2)}) copy-start(f32[2,8,16,256]{3,2,1,0:T(8,128)} %right.1) | copy-start | bytes 786436
  1.8 11.1 %collective-permute-start.1 = (f32[3,8,3,256]{3,2,1,0:T(4,128)S(1)}, f32[3,8,3,256]{3,2,1,0:T(4,128)S(1)}, u32[]{:S(2)}, u32[]{:S(2)}) collective-permute-start(f32[3,8,3,256]{3,2,1,0:T(4,128)S(1)} %broadcast_select_fusion.6), channel_id=1, source_target_pairs={{0,1},{2,3},{4,5},{6,7},{8,9},{10,11},{12,13},{14,15},{16,17},{18,... | collective-permute-start | bytes 221192 | tf_op jit(solution)/shard_map/ppermute | solution.py:479
  10.7 10.0 %copy-start.1 = (f32[8,16,256]{2,1,0:T(8,128)S(1)}, f32[8,16,256]{2,1,0:T(8,128)}, u32[]{:S(2)}) copy-start(f32[8,16,256]{2,1,0:T(8,128)} %param.3) | copy-start | bytes 393220
  10.7 10.0 %collective-permute-start = (f32[3,8,3,256]{3,2,1,0:T(4,128)S(1)}, f32[3,8,3,256]{3,2,1,0:T(4,128)S(1)}, u32[]{:S(2)}, u32[]{:S(2)}) collective-permute-start(f32[3,8,3,256]{3,2,1,0:T(4,128)S(1)} %get-tuple-element.35), channel_id=1, source_target_pairs={{1,2},{3,4},{5,6},{7,8},{9,10},{11,12},{13,14},{15,16},{17,18},{19... | collective-permute-start | bytes 221192 | tf_op jit(solution)/shard_map/ppermute | solution.py:478
  21.0 4.2 %collective-permute-start.2 = (f32[3,3,24,256]{3,2,1,0:T(8,128)S(1)}, f32[3,3,24,256]{3,2,1,0:T(8,128)S(1)}, u32[]{:S(2)}, u32[]{:S(2)}) collective-permute-start(f32[3,3,24,256]{3,2,1,0:T(8,128)S(1)} %get-tuple-element.38), channel_id=1, source_target_pairs={{0,32},{32,64},{64,96},{96,128},{128,160},{160,192},{192,224},{224... | collective-permute-start | bytes 663560 | tf_op jit(solution)/shard_map/ppermute | solution.py:487
  22.3 6.7 %collective-permute-start.3 = (f32[3,3,24,256]{3,2,1,0:T(8,128)S(1)}, f32[3,3,24,256]{3,2,1,0:T(8,128)S(1)}, u32[]{:S(2)}, u32[]{:S(2)}) collective-permute-start(f32[3,3,24,256]{3,2,1,0:T(8,128)S(1)} %get-tuple-element.39), channel_id=1, source_target_pairs={{32,0},{64,32},{96,64},{128,96},{160,128},{192,160},{224,192},{256... | collective-permute-start | bytes 663560 | tf_op jit(solution)/shard_map/ppermute | solution.py:487
  32.2 21.5 %collective-permute-start.4 = (f32[3,2,8,128]{3,2,1,0:T(8,128)S(1)}, f32[3,2,8,128]{3,2,1,0:T(8,128)S(1)}, u32[]{:S(2)}, u32[]{:S(2)}) collective-permute-start(f32[3,2,8,128]{3,2,1,0:T(8,128)S(1)} %get-tuple-element.21), channel_id=1, source_target_pairs={{1,2},{3,4},{5,6},{7,8},{9,10},{11,12},{13,14},{15,16},{17,18},{19... | collective-permute-start | bytes 73736 | tf_op jit(solution)/shard_map/ppermute | solution.py:478
  38.8 14.8 %collective-permute-start.5 = (f32[3,2,8,128]{3,2,1,0:T(8,128)S(1)}, f32[3,2,8,128]{3,2,1,0:T(8,128)S(1)}, u32[]{:S(2)}, u32[]{:S(2)}) collective-permute-start(f32[3,2,8,128]{3,2,1,0:T(8,128)S(1)} %get-tuple-element.22), channel_id=1, source_target_pairs={{0,1},{2,3},{4,5},{6,7},{8,9},{10,11},{12,13},{14,15},{16,17},{18,... | collective-permute-start | bytes 73736 | tf_op jit(solution)/shard_map/ppermute | solution.py:479
  40.8 24.5 %all-to-all-start = ((f32[32,1,128]{2,1,0:T(1,128)}), f32[32,1,128]{2,1,0:T(1,128)S(1)}, u32[]{:S(2)}, u32[]{:S(2)}) async-start(f32[32,1,128]{2,1,0:T(1,128)} %get-tuple-element.19), calls=%async_computation | async-start | bytes 32768 | tf_op jit(solution)/shard_map/all_to_all | solution.py:534
  66.1 16.8 %all-to-all-start.1 = ((f32[16,16,128]{2,1,0:T(8,128)}), f32[16,16,128]{2,1,0:T(8,128)S(1)}, u32[]{:S(2)}, u32[]{:S(2)}) async-start(f32[16,16,128]{2,1,0:T(8,128)} %broadcast_in_dim.7), calls=%async_computation.1 | async-start | bytes 262144 | tf_op jit(solution)/shard_map/all_to_all | solution.py:542
  75.1 6.3 %collective-permute-start.7 = (f32[3,4,16,128]{3,2,1,0:T(8,128)S(1)}, f32[3,4,16,128]{3,2,1,0:T(8,128)S(1)}, u32[]{:S(2)}, u32[]{:S(2)}) collective-permute-start(f32[3,4,16,128]{3,2,1,0:T(8,128)S(1)} %pad_maximum_fusion.8), channel_id=1, source_target_pairs={{32,0},{64,32},{96,64},{128,96},{160,128},{192,160},{224,192},{256... | collective-permute-start | bytes 294920 | tf_op jit(solution)/shard_map/ppermute | solution.py:487
  76.4 5.6 %collective-permute-start.6 = (f32[3,4,16,128]{3,2,1,0:T(8,128)S(1)}, f32[3,4,16,128]{3,2,1,0:T(8,128)S(1)}, u32[]{:S(2)}, u32[]{:S(2)}) collective-permute-start(f32[3,4,16,128]{3,2,1,0:T(8,128)S(1)} %pad_maximum_fusion.8), channel_id=1, source_target_pairs={{0,32},{32,64},{64,96},{96,128},{128,160},{160,192},{192,224},{224... | collective-permute-start | bytes 294920 | tf_op jit(solution)/shard_map/ppermute | solution.py:487
  86.6 10.2 %collective-permute-start.8 = (f32[2,8,16,128]{3,2,1,0:T(8,128)S(1)}, f32[2,8,16,128]{3,2,1,0:T(8,128)S(1)}, u32[]{:S(2)}, u32[]{:S(2)}) collective-permute-start(f32[2,8,16,128]{3,2,1,0:T(8,128)S(1)} %get-tuple-element.50), channel_id=1, source_target_pairs={{1,2},{3,4},{5,6},{7,8},{9,10},{11,12},{13,14},{15,16},{17,18},{19... | collective-permute-start | bytes 393224 | tf_op jit(solution)/shard_map/ppermute | solution.py:478
  90.9 5.8 %collective-permute-start.9 = (f32[2,8,16,128]{3,2,1,0:T(8,128)S(1)}, f32[2,8,16,128]{3,2,1,0:T(8,128)S(1)}, u32[]{:S(2)}, u32[]{:S(2)}) collective-permute-start(f32[2,8,16,128]{3,2,1,0:T(8,128)S(1)} %get-tuple-element.51), channel_id=1, source_target_pairs={{0,1},{2,3},{4,5},{6,7},{8,9},{10,11},{12,13},{14,15},{16,17},{18,... | collective-permute-start | bytes 393224 | tf_op jit(solution)/shard_map/ppermute | solution.py:479
  97.0 7.9 %collective-permute-start.11 = (f32[2,4,64,128]{3,2,1,0:T(8,128)S(1)}, f32[2,4,64,128]{3,2,1,0:T(8,128)S(1)}, u32[]{:S(2)}, u32[]{:S(2)}) collective-permute-start(f32[2,4,64,128]{3,2,1,0:T(8,128)S(1)} %pad_maximum_fusion.3), channel_id=1, source_target_pairs={{32,0},{64,32},{96,64},{128,96},{160,128},{192,160},{224,192},{256... | collective-permute-start | bytes 786440 | tf_op jit(solution)/shard_map/ppermute | solution.py:487
  98.4 8.4 %collective-permute-start.10 = (f32[2,4,64,128]{3,2,1,0:T(8,128)S(1)}, f32[2,4,64,128]{3,2,1,0:T(8,128)S(1)}, u32[]{:S(2)}, u32[]{:S(2)}) collective-permute-start(f32[2,4,64,128]{3,2,1,0:T(8,128)S(1)} %pad_maximum_fusion.2), channel_id=1, source_target_pairs={{0,32},{32,64},{64,96},{96,128},{128,160},{160,192},{192,224},{224... | collective-permute-start | bytes 786440 | tf_op jit(solution)/shard_map/ppermute | solution.py:487
  108.8 19.5 %all-to-all-start.2 = ((f32[32,1,128]{2,1,0:T(1,128)}), f32[32,1,128]{2,1,0:T(1,128)S(1)}, u32[]{:S(2)}, u32[]{:S(2)}) async-start(f32[32,1,128]{2,1,0:T(1,128)} %get-tuple-element.29), calls=%async_computation.2 | async-start | bytes 32768 | tf_op jit(solution)/shard_map/all_to_all | solution.py:534
  116.7 11.8 %collective-permute-start.13 = (f32[2,2,16,128]{3,2,1,0:T(8,128)S(1)}, f32[2,2,16,128]{3,2,1,0:T(8,128)S(1)}, u32[]{:S(2)}, u32[]{:S(2)}) collective-permute-start(f32[2,2,16,128]{3,2,1,0:T(8,128)S(1)} %slice.172), channel_id=1, source_target_pairs={{32,0},{64,32},{96,64},{128,96},{160,128},{192,160},{224,192},{256... | collective-permute-start | bytes 98312 | tf_op jit(solution)/shard_map/ppermute | solution.py:487
  118.0 10.5 %collective-permute-start.12 = (f32[2,2,16,128]{3,2,1,0:T(8,128)S(1)}, f32[2,2,16,128]{3,2,1,0:T(8,128)S(1)}, u32[]{:S(2)}, u32[]{:S(2)}) collective-permute-start(f32[2,2,16,128]{3,2,1,0:T(8,128)S(1)} %slice.172), channel_id=1, source_target_pairs={{0,32},{32,64},{64,96},{96,128},{128,160},{160,192},{192,224},{224... | collective-permute-start | bytes 98312 | tf_op jit(solution)/shard_map/ppermute | solution.py:487
